TPU v7x, 32 devices: a whole 2x2x4 slice. The times are simulated.
32 devices in a mesh: groups: 2 (over x), ctx: 16 (over z, y, core).
Axes of the slice: x: 2, y: 2, z: 4, core: 2. Of those that a mesh axis runs over, the one named last changes fastest.
Arguments:
- hidden_in: bfloat16 [32, 8192], P('groups', 'ctx'), parts along dimension 0, may hold values from -6 to 6
- attn_gain: float32 [8192], replicated, may hold values from 0.1 to 1.9
- w_query: bfloat16 [8192, 4096], P(None, 'ctx'), may hold values from -0.0625 to 0.0625
- w_key: bfloat16 [8192, 512], P(None, 'ctx'), may hold values from -0.375 to 0.375
- w_value: bfloat16 [8192, 512], P(None, 'ctx'), may hold values from -0.0625 to 0.0625
- rotated_prefix_keys: bfloat16 [32768, 4, 128], P(('groups', 'ctx')), parts along dimension 0, may hold values from -70 to 70
- cache_values: bfloat16 [32768, 4, 128], P(('groups', 'ctx')), parts along dimension 0, may hold values from -6 to 6
- w_out: bfloat16 [4096, 8192], P(None, 'ctx'), may hold values from -0.09375 to 0.09375
- ffn_gain: float32 [8192], replicated, may hold values from 0.1 to 1.9
- w_gate: bfloat16 [8192, 14336], P(None, 'ctx'), may hold values from -0.0625 to 0.0625
- w_up: bfloat16 [8192, 14336], P(None, 'ctx'), may hold values from -0.0625 to 0.0625
- w_down: bfloat16 [14336, 8192], P(None, 'ctx'), may hold values from -0.046875 to 0.046875
- doc_offsets: int32 [32], P('groups'), parts along dimension 0, may hold values from 8192 to 16384
- slot_request: int32 [32], P('groups'), parts along dimension 0, may hold values from 0 to 15, each once
Outputs:
- layer_out: bfloat16 [32, 8192], P('groups', 'ctx'), parts along dimension 0
There are 2 independent parts, one for each index of `groups`. A program takes and returns all parts, laid end to end along the dimension named above; an argument that names none is the same for every part. Nothing has to cross between parts.
Inputs may be any that keep to these rules, and one draw needn't show every extreme that they name: `slot_request`: each slot holds a different request.
All inputs are finite; a program needn't handle non-finite values.
Results may differ from a plain program's by a relative error of at most 0.011.
Values may be sent and summed in bfloat16 or wider, within the bound.
A program may use at most 128 MiB of HBM per device.

v0:
```python
import math

import jax
import jax.numpy as jnp
from jax import lax
from jax.sharding import PartitionSpec as P

NORM_EPSILON = 1e-05
ROPE_BASE = 500000.0
MASKED = -1e30


def joined(part, axis, combine):
    gathered = jax.tree.map(lambda a: lax.all_gather(a, axis), part)

    def take(source):
        return jax.tree.map(lambda a: lax.dynamic_index_in_dim(a, source, 0, False), gathered)

    return lax.fori_loop(
        1, lax.axis_size(axis), lambda source, state: combine(state, take(source)), take(0)
    )


def rms_norm(values, gain_row):
    wide_rows = values.astype(jnp.float32)
    factor = lax.rsqrt(jnp.mean(wide_rows * wide_rows, axis=1, keepdims=True) + NORM_EPSILON)
    return (wide_rows * factor * gain_row[None, :]).astype(jnp.bfloat16)


def rotate(columns, first_col, positions, head_dim):
    col_count = columns.shape[1]
    pair_cols = first_col + jnp.arange(col_count // 2, dtype=jnp.int32) * 2
    in_head = (pair_cols % head_dim).astype(jnp.float32)
    frequency = jnp.exp(-(in_head / head_dim) * jnp.log(jnp.float32(ROPE_BASE)))
    angles = positions.astype(jnp.float32)[:, None] * frequency[None, :]
    paired = columns.reshape(columns.shape[0], col_count // 2, 2)
    even_part = paired[..., 0]
    odd_part = paired[..., 1]
    cosine = jnp.cos(angles)
    sine = jnp.sin(angles)
    turned = jnp.stack(
        [even_part * cosine - odd_part * sine, even_part * sine + odd_part * cosine], axis=-1
    )
    return turned.reshape(columns.shape)


def combine_parts(first_part, second_part):
    top_first, total_first, accum_first = first_part
    top_second, total_second, accum_second = second_part
    peak_score = jnp.maximum(top_first, top_second)
    share_first = jnp.exp(top_first - peak_score)
    share_second = jnp.exp(top_second - peak_score)
    merged_total = total_first * share_first + total_second * share_second
    merged_accum = accum_first * share_first[..., None] + accum_second * share_second[..., None]
    return (peak_score, merged_total, merged_accum)


def shards(
    hidden_in,
    attn_gain,
    w_query,
    w_key,
    w_value,
    rotated_prefix_keys,
    cache_values,
    w_out,
    ffn_gain,
    w_gate,
    w_up,
    w_down,
    doc_offsets,
    slot_request,
):
    devices = lax.axis_size("ctx")
    device = lax.axis_index("ctx")
    batch_rows = hidden_in.shape[0]
    block_span, value_heads, head_dim = rotated_prefix_keys.shape
    query_width = w_query.shape[1]
    key_width = w_key.shape[1]
    head_count = query_width * devices // head_dim
    group_size = head_count // value_heads
    logit_scale_factor = 1.0 / math.sqrt(head_dim)
    slot_index = jnp.arange(batch_rows, dtype=jnp.int32)
    positions = jnp.sum(
        jnp.where(slot_request[:, None] == slot_index[None, :], doc_offsets[None, :], 0), axis=1
    )
    full_rows = lax.all_gather(hidden_in, "ctx", axis=1, tiled=True)
    normed = rms_norm(full_rows, attn_gain)
    query_part = rotate(
        jnp.dot(normed, w_query, preferred_element_type=jnp.float32),
        device * query_width,
        positions,
        head_dim,
    ).astype(jnp.bfloat16)
    key_part = rotate(
        jnp.dot(normed, w_key, preferred_element_type=jnp.float32),
        device * key_width,
        positions,
        head_dim,
    ).astype(jnp.bfloat16)
    value_part = jnp.dot(normed, w_value, preferred_element_type=jnp.float32).astype(jnp.bfloat16)
    queries, key_new, value_new = (
        lax.all_gather(query_part, "ctx", axis=1, tiled=True),
        lax.all_gather(key_part, "ctx", axis=1, tiled=True),
        lax.all_gather(value_part, "ctx", axis=1, tiled=True),
    )
    query_groups = queries.reshape(batch_rows, value_heads, group_size, head_dim)
    attention_logits = (
        jnp.einsum(
            "owqa,zwa->owqz", query_groups, rotated_prefix_keys, preferred_element_type=jnp.float32
        )
        * logit_scale_factor
    )
    places = device * block_span + jnp.arange(block_span, dtype=jnp.int32)
    visible = (places[None, :] < positions[:, None])[:, None, None, :]
    masked = jnp.where(visible, attention_logits, MASKED)
    block_top = jnp.max(masked, axis=3)
    weights = jnp.where(visible, jnp.exp(masked - block_top[..., None]), 0.0)
    block_total = jnp.sum(weights, axis=3)
    block_value_sum = jnp.einsum(
        "nelw,weh->nelh",
        weights.astype(jnp.bfloat16),
        cache_values,
        preferred_element_type=jnp.float32,
    )
    own_score = (
        jnp.einsum(
            "rkgd,rkd->rkg",
            query_groups,
            key_new.reshape(batch_rows, value_heads, head_dim),
            preferred_element_type=jnp.float32,
        )
        * logit_scale_factor
    ).reshape(batch_rows, head_count)
    spread_value = jnp.broadcast_to(
        value_new.reshape(batch_rows, value_heads, 1, head_dim),
        (batch_rows, value_heads, group_size, head_dim),
    ).reshape(batch_rows, head_count * head_dim)
    global_top, global_total, prefix_accum = joined(
        (block_top, block_total, block_value_sum), "ctx", combine_parts
    )
    finish_global_top = global_top
    finish_global_total = global_total
    finish_global_top = finish_global_top.reshape(batch_rows, head_count)
    finish_global_total = finish_global_total.reshape(batch_rows, head_count)
    peak_score = jnp.maximum(finish_global_top, own_score)
    kept_share = jnp.exp(finish_global_top - peak_score)
    fresh_share = jnp.exp(own_score - peak_score)
    denominator = finish_global_total * kept_share + fresh_share

    def columns(per_head):
        return jnp.repeat(per_head, head_dim, axis=1)

    value_cols = spread_value.astype(jnp.float32)
    attn_all = (
        (
            prefix_accum.reshape(batch_rows, head_count * head_dim) * columns(kept_share)
            + columns(fresh_share) * value_cols
        )
        / columns(denominator)
    ).astype(jnp.bfloat16)
    attn_part = jnp.dot(attn_all, w_out, preferred_element_type=jnp.float32)
    mid_part = (hidden_in.astype(jnp.float32) + attn_part).astype(jnp.bfloat16)
    mid_full = lax.all_gather(mid_part, "ctx", axis=1, tiled=True)
    normed_mid = rms_norm(mid_full, ffn_gain)
    gate_act = jnp.dot(normed_mid, w_gate, preferred_element_type=jnp.float32)
    up_act = jnp.dot(normed_mid, w_up, preferred_element_type=jnp.float32)
    hidden = (jax.nn.silu(gate_act) * up_act).astype(jnp.bfloat16)
    down_part = jnp.dot(
        lax.all_gather(hidden, "ctx", axis=1, tiled=True),
        w_down,
        preferred_element_type=jnp.float32,
    )
    return (mid_part.astype(jnp.float32) + down_part).astype(jnp.bfloat16)


def solution(mesh):
    return jax.shard_map(
        shards,
        mesh=mesh,
        in_specs=(
            P("groups", "ctx"),
            P(),
            P(None, "ctx"),
            P(None, "ctx"),
            P(None, "ctx"),
            P(("groups", "ctx"), None, None),
            P(("groups", "ctx"), None, None),
            P(None, "ctx"),
            P(),
            P(None, "ctx"),
            P(None, "ctx"),
            P(None, "ctx"),
            P("groups"),
            P("groups"),
        ),
        out_specs=P("groups", "ctx"),
        check_vma=False,
    )
```

profile of v0, /device:TPU:0, one launch (start us, length us, event | category | flops | bytes accessed | tf_op | source)
XLA Modules:
  0.0 229.3 jit_solution(7356914629997899854)
XLA Ops:
  6.6 0.9 select_reduce_fusion
  7.6 24.1 %all_gather.36 = bf16[16,8192]{1,0:T(8,128)(2,1)S(1)} all-gather(bf16[16,512]{1,0:T(8,128)(2,1)} %param.16), channel_id=1, replica_groups=mesh['groups'=2,'ctx'=16] {'ctx'}, dimensions={1}, use_global_device_ids=true | all-gather | bytes 278528 | tf_op jit(solution)/shard_map/all_gather | solution.py:87
  31.7 0.2 fusion.22
  31.9 4.0 %fusion.71 = f32[16,256]{0,1:T(8,128)S(1)} fusion(bf16[8192,256]{1,0:T(8,128)(2,1)} %param.18, bf16[16,8192]{1,0:T(8,128)(2,1)S(1)} %all_gather.36, f32[8192]{0:T(1024)} %param.17, f32[16]{0:T(128)S(1)} %add_rsqrt_fusion.1), kind=kOutput, calls=%fused_computation.108 | convolution fusion | flops 67633152 | bytes 4505664 | tf_op jit(solution)/shard_map/dot_general | solution.py:90
  36.1 0.1 fusion.50
  36.2 0.1 copy.106
  36.3 20.5 %all_gather.37 = bf16[16,4096]{0,1:T(8,128)(2,1)S(1)} all-gather(bf16[16,256]{0,1:T(8,128)(2,1)S(1)} %bitcast.138), channel_id=1, replica_groups=mesh['groups'=2,'ctx'=16] {'ctx'}, dimensions={1}, use_global_device_ids=true | all-gather | bytes 139264 | tf_op jit(solution)/shard_map/all_gather | solution.py:103
  56.8 0.3 copy.108
  57.2 0.7 bitcast_reduce_fusion
  57.9 1.3 copy-done.2
  59.2 1.7 convolution_bitcast_fusion
  61.0 0.4 copy.137
  61.5 1.6 fusion.69
  63.5 20.0 %all-gather.3 = bf16[16,32,16]{1,2,0:T(8,128)(2,1)S(1)} all-gather(bf16[1,32,16]{1,2,0:T(8,128)(2,1)S(1)} %copy.125), channel_id=1, replica_groups=mesh['groups'=2,'ctx'=16] {'ctx'}, dimensions={0}, use_global_device_ids=true | all-gather | bytes 17408 | tf_op jit(solution)/shard_map/all_gather | solution.py:104
  83.7 0.3 fusion.11
  84.0 18.1 %all-gather.4 = bf16[16,32,16]{1,2,0:T(8,128)(2,1)S(1)} all-gather(bf16[1,32,16]{1,2,0:T(8,128)(2,1)S(1)} %fusion.11), channel_id=1, replica_groups=mesh['groups'=2,'ctx'=16] {'ctx'}, dimensions={0}, use_global_device_ids=true | all-gather | bytes 17408 | tf_op jit(solution)/shard_map/all_gather | solution.py:105
  102.2 0.2 fusion.78
  102.5 0.8 fusion.7
  103.3 20.8 %all-gather.1 = f32[256,4,8]{2,1,0:T(4,128)S(1)} all-gather(f32[16,4,8]{2,1,0:T(4,128)S(1)} %copy.111), channel_id=3, replica_groups=mesh['groups'=2,'ctx'=16] {'ctx'}, dimensions={0}, use_global_device_ids=true | all-gather | bytes 34816 | tf_op jit(solution)/shard_map/all_gather | solution.py:14
  124.3 0.2 copy.119
  124.5 19.1 %all-gather = f32[256,4,8]{2,1,0:T(4,128)S(1)} all-gather(f32[16,4,8]{2,1,0:T(4,128)S(1)} %copy.110), channel_id=2, replica_groups=mesh['groups'=2,'ctx'=16] {'ctx'}, dimensions={0}, use_global_device_ids=true | all-gather | bytes 34816 | tf_op jit(solution)/shard_map/all_gather | solution.py:14
  143.6 0.2 copy.118
  143.8 1.0 slice.26
  144.8 21.4 %while.19 = (s32[]{:T(128)}, f32[16,4,8]{0,2,1:T(8,128)S(1)}, f32[16,4,8]{0,2,1:T(8,128)S(1)}, f32[16,4,8,128]{3,2,1,0:T(8,128)S(1)}, f32[16,16,4,8]{1,3,2,0:T(8...) while((s32[]{:T(128)}, f32[16,4,8]{0,2,1:T(8,128)S(1)}, ...), condition=%wide.region_5.6_spmd, body=%wide.region_4.5_spmd.sunk | while | flops 199685 | bytes 815247 | solution.py:19
  145.0 1.2 fusion.93
  146.5 1.2 fusion.93
  147.9 1.2 fusion.93
  149.3 1.2 fusion.93
  150.7 1.2 fusion.93
  152.2 1.2 fusion.93
  153.6 1.2 fusion.93
  155.0 1.2 fusion.93
  156.5 1.2 fusion.93
  157.9 1.2 fusion.93
  159.3 1.2 fusion.93
  160.7 1.2 fusion.93
  162.2 1.2 fusion.93
  163.6 1.2 fusion.93
  165.0 1.2 fusion.93
  167.0 3.8 %fusion.10 = bf16[16,512]{1,0:T(8,128)(2,1)S(1)} fusion(bf16[4096,512]{1,0:T(8,128)(2,1)} %param.23, f32[2,8,32,128]{3,2,1,0:T(8,128)S(1)} %bitcast.135, f32[2,8,32,128]{3,2,1,0:T(8,128)S(1)} %bitcast.132, f32[2,8,32,128]{3,2,1,0:T(8,128)S(1)} %bitcast.133, f32[2,8,32,128]{3,2,1,0:T(8,128)S(1)} %bitcast.134, f32[2,8,32,128]{3,2,1,0:T(8,128)S(1)} %bitcast.127, ...), kind=kOutput, calls=%fused_computation.23 | convolution fusion | flops 67461120 | bytes 5537792 | tf_op jit(solution)/shard_map/dot_general | solution.py:162
  170.7 19.5 %all_gather.46 = bf16[16,8192]{1,0:T(8,128)(2,1)S(1)} all-gather(bf16[16,512]{1,0:T(8,128)(2,1)S(1)} %fusion.10), channel_id=1, replica_groups=mesh['groups'=2,'ctx'=16] {'ctx'}, dimensions={1}, use_global_device_ids=true | all-gather | bytes 278528 | tf_op jit(solution)/shard_map/all_gather | solution.py:164
  190.3 0.2 fusion.25
  190.5 7.4 %fusion.32 = f32[16,896]{1,0:T(8,128)S(1)} fusion(bf16[8192,896]{1,0:T(8,128)(2,1)} %param.25, bf16[16,8192]{1,0:T(8,128)(2,1)S(1)} %all_gather.46, f32[8192]{0:T(1024)S(1)} %copy-done.4, f32[16]{0:T(128)S(1)} %add_rsqrt_fusion), kind=kOutput, calls=%fused_computation.50 | convolution fusion | flops 235405312 | bytes 15032384 | tf_op jit(solution)/shard_map/dot_general | solution.py:166
  197.9 0.2 slice-done.2
  198.1 0.6 slice-done.3
  198.7 2.0 fusion.8
  200.7 19.1 %all_gather.47 = bf16[16,14336]{1,0:T(8,128)(2,1)S(1)} all-gather(bf16[16,896]{1,0:T(8,128)(2,1)S(1)} %fusion.8), channel_id=1, replica_groups=mesh['groups'=2,'ctx'=16] {'ctx'}, dimensions={1}, use_global_device_ids=true | all-gather | bytes 487424 | tf_op jit(solution)/shard_map/all_gather | solution.py:170
  219.8 2.6 %fusion.9 = bf16[16,512]{1,0:T(8,128)(2,1)} fusion(bf16[16,14336]{1,0:T(8,128)(2,1)S(1)} %all_gather.47, bf16[14336,512]{1,0:T(8,128)(2,1)S(1)} %bitcast.126, bf16[16,512]{1,0:T(8,128)(2,1)S(1)} %fusion.10), kind=kOutput, calls=%fused_computation.22 | convolution fusion | flops 234905600 | bytes 15171584 | tf_op jit(solution)/shard_map/dot_general | solution.py:169
  (121 shorter events, 4.9 us)
Async XLA Ops:
  6.5 50.7 %copy-start = (bf16[1024,4,128]{2,1,0:T(4,128)(2,1)S(1)}, bf16[1024,4,128]{2,1,0:T(4,128)(2,1)}, u32[]{:S(2)}) copy-start(bf16[1024,4,128]{2,1,0:T(4,128)(2,1)} %param.21) | copy-start | bytes 3145732
  6.5 137.3 %all-gather.7.cloned.1.call-start = ((), (), s32[]{:S(2)}) async-start(), calls=%async_computation | async-start | bytes 4456448 | tf_op jit(solution)/shard_map/all_gather | solution.py:14
  57.2 2.0 copy-start.8
  57.9 1.4 copy-start.2
  59.2 2.2 copy-start.6
  61.0 22.7 %copy-start.5 = (bf16[8192,32]{0,1:T(8,128)(2,1)S(1)}, bf16[8192,32]{0,1:T(8,128)(2,1)}, u32[]{:S(2)}) copy-start(bf16[8192,32]{0,1:T(8,128)(2,1)} %param.20) | copy-start | bytes 1572868
  61.4 41.1 %copy-start.3 = (f32[4,16,8,1024]{3,2,1,0:T(8,128)S(1)}, f32[4,16,8,1024]{3,2,1,0:T(8,128)}, u32[]{:S(2)}) copy-start(f32[4,16,8,1024]{3,2,1,0:T(8,128)} %copy-done.2) | copy-start | bytes 6291460
  144.8 22.1 %copy-start.7 = (bf16[16,512]{1,0:T(8,128)(2,1)S(1)}, bf16[16,512]{1,0:T(8,128)(2,1)}, u32[]{:S(2)}) copy-start(bf16[16,512]{1,0:T(8,128)(2,1)} %param.16) | copy-start | bytes 49156
  166.9 23.5 %copy-start.4 = (f32[8192]{0:T(1024)S(1)}, f32[8192]{0:T(1024)}, u32[]{:S(2)}) copy-start(f32[8192]{0:T(1024)} %param.24) | copy-start | bytes 98308
  166.9 30.9 %slice-start = ((s8[14680064]{0:T(1024)(128)(4,1)}), s8[4194304]{0:T(1024)(128)(4,1)S(1)}, s32[]{:S(2)}) async-start(s8[14680064]{0:T(1024)(128)(4,1)} %bitcast.123), calls=%async_computation.1 | async-start | bytes 8388608
  190.5 7.4 %slice-start.1 = ((s8[14680064]{0:T(1024)(128)(4,1)}), s8[4194304]{0:T(1024)(128)(4,1)S(1)}, s32[]{:S(2)}) async-start(s8[14680064]{0:T(1024)(128)(4,1)} %bitcast.123), calls=%async_computation.2 | async-start | bytes 8388608
  190.5 7.6 %slice-start.2 = ((s8[14680064]{0:T(1024)(128)(4,1)}), s8[4194304]{0:T(1024)(128)(4,1)S(1)}, s32[]{:S(2)}) async-start(s8[14680064]{0:T(1024)(128)(4,1)} %bitcast.123), calls=%async_computation.3 | async-start | bytes 8388608
  190.5 8.2 %slice-start.3 = ((s8[14680064]{0:T(1024)(128)(4,1)}), s8[2097152]{0:T(1024)(128)(4,1)S(1)}, s32[]{:S(2)}) async-start(s8[14680064]{0:T(1024)(128)(4,1)} %bitcast.123), calls=%async_computation.4 | async-start | bytes 4194304
  190.5 29.3 %slice-start.4 = ((s8[14680064]{0:T(1024)(128)(4,1)}), s8[4194304]{0:T(1024)(128)(4,1)S(1)}, s32[]{:S(2)}) async-start(s8[14680064]{0:T(1024)(128)(4,1)} %bitcast.125), calls=%async_computation.5 | async-start | bytes 8388608
  190.5 29.3 %slice-start.5 = ((s8[14680064]{0:T(1024)(128)(4,1)}), s8[4194304]{0:T(1024)(128)(4,1)S(1)}, s32[]{:S(2)}) async-start(s8[14680064]{0:T(1024)(128)(4,1)} %bitcast.125), calls=%async_computation.6 | async-start | bytes 8388608
  198.7 21.1 %slice-start.6 = ((s8[14680064]{0:T(1024)(128)(4,1)}), s8[4194304]{0:T(1024)(128)(4,1)S(1)}, s32[]{:S(2)}) async-start(s8[14680064]{0:T(1024)(128)(4,1)} %bitcast.125), calls=%async_computation.7 | async-start | bytes 8388608
  198.7 21.1 %slice-start.7 = ((s8[14680064]{0:T(1024)(128)(4,1)}), s8[2097152]{0:T(1024)(128)(4,1)S(1)}, s32[]{:S(2)}) async-start(s8[14680064]{0:T(1024)(128)(4,1)} %bitcast.125), calls=%async_computation.8 | async-start | bytes 4194304
  219.8 2.6 %copy-start.1 = (bf16[1024,4,128]{2,1,0:T(4,128)(2,1)S(1)}, bf16[1024,4,128]{2,1,0:T(4,128)(2,1)}, u32[]{:S(2)}) copy-start(bf16[1024,4,128]{2,1,0:T(4,128)(2,1)} %param.21) | copy-start | bytes 3145732
Sparse Core Ops, SparseCore 0:
  61.1 51.8 all-gather.6
where the time goes:
time: 230 us; the launch traced here: 229 us
  blocking collectives  161 us (70%)
  matrix products  24.2 us (11%)
  other arithmetic  21.2 us (9%)
  between operations  13.7 us (6%)
  local copies, waits for them, and re-layouts  8.55 us (4%)
    all_gather x2, blocking collectives, joined(): gathered = jax.tree.map(lambda a: lax.all_gather(a, axis), part)  39.9 us
    all_gather x1, blocking collectives, shards(): full_rows = lax.all_gather(hidden_in, 'ctx', axis=1, tiled=True)  24.1 us
    all_gather x1, blocking collectives, shards(): lax.all_gather(query_part, 'ctx', axis=1, tiled=True)  20.5 us
    all_gather x1, blocking collectives, shards(): lax.all_gather(key_part, 'ctx', axis=1, tiled=True)  20 us
    all_gather x1, blocking collectives, shards(): mid_full = lax.all_gather(mid_part, 'ctx', axis=1, tiled=True)  19.5 us
    all_gather x1, blocking collectives, shards(): lax.all_gather(hidden, 'ctx', axis=1, tiled=True)  19.1 us
    add x15, other arithmetic, combine_parts(): accum_first * share_first[..., None]  18.2 us
    all_gather x1, blocking collectives, shards(): lax.all_gather(value_part, 'ctx', axis=1, tiled=True)  18.1 us
  transfers between devices with their start and end apart: 1, of which 0 were waited for; matrix products, arithmetic and copies ran while one was open for 2% of the time, Pallas kernels for 0%

commit v1 on v0

--- a/solution.py
+++ b/solution.py
@@ -1,8 +1,11 @@
+import functools
 import math
 
 import jax
 import jax.numpy as jnp
 from jax import lax
+from jax.experimental import pallas as pl
+from jax.experimental.pallas import tpu as pltpu
 from jax.sharding import PartitionSpec as P
 
 NORM_EPSILON = 1e-05
@@ -55,7 +58,7 @@
     return (peak_score, merged_total, merged_accum)
 
 
-def shards(
+def plain_shards(
     hidden_in,
     attn_gain,
     w_query,
@@ -174,9 +177,452 @@
     return (mid_part.astype(jnp.float32) + down_part).astype(jnp.bfloat16)
 
 
+MESH = pl.DeviceIdType.MESH
+F32 = jnp.float32
+BF16 = jnp.bfloat16
+
+
+def dot(a, b):
+    return jnp.dot(a, b, preferred_element_type=F32)
+
+
+def dot_nt(a, b):
+    return lax.dot_general(a, b, (((1,), (1,)), ((), ())), preferred_element_type=F32)
+
+
+def turn(x, cosine, signed_sine):
+    lane = lax.broadcasted_iota(jnp.int32, x.shape, 1)
+    after = pltpu.roll(x, x.shape[1] - 1, 1)
+    before = pltpu.roll(x, 1, 1)
+    return x * cosine + jnp.where(lane % 2 == 0, after, before) * signed_sine
+
+
+def three_terms(x):
+    high = x.astype(BF16).astype(F32)
+    left = x - high
+    mid = left.astype(BF16).astype(F32)
+    return high, mid, left - mid
+
+
+def layer_kernel(
+    n,
+    hidden_ref,
+    again_ref,
+    fgain_ref,
+    table_ref,
+    place_ref,
+    wq_hbm,
+    wk_hbm,
+    wv_hbm,
+    keys_hbm,
+    values_hbm,
+    wo_hbm,
+    wg_hbm,
+    wu_hbm,
+    wd_hbm,
+    out_ref,
+    wq,
+    wkv,
+    keys,
+    values,
+    wo,
+    wg,
+    wu,
+    wd,
+    xbuf,
+    qbuf,
+    asend,
+    arecv,
+    abuf,
+    mbuf,
+    hbuf,
+    nbuf,
+    local_sem,
+    send_sem,
+    recv_sem,
+):
+    me = lax.axis_index("ctx")
+    rows = hidden_ref.shape[0]
+    kv_heads, span, head_dim = keys.shape
+    q_width = wq.shape[2]
+    k_width = wk_hbm.shape[0]
+    own_heads = q_width // head_dim
+    head_count = own_heads * n
+    group = head_count // kv_heads
+    stat_lanes = head_dim // own_heads
+    scale = 1.0 / math.sqrt(head_dim)
+
+    loads = [
+        pltpu.make_async_copy(source, target, local_sem.at[i])
+        for i, (source, target) in enumerate(
+            [
+                (wq_hbm, wq),
+                (wk_hbm, wkv.at[pl.ds(0, k_width)]),
+                (wv_hbm, wkv.at[pl.ds(k_width, k_width)]),
+                (keys_hbm, keys),
+                (values_hbm, values),
+                (wo_hbm, wo),
+                (wg_hbm, wg),
+                (wu_hbm, wu),
+                (wd_hbm, wd),
+            ]
+        )
+    ]
+    for load in loads:
+        load.start()
+
+    barrier = pltpu.get_barrier_semaphore()
+
+    @pl.loop(1, n)
+    def _(i):
+        pl.semaphore_signal(
+            barrier, inc=1, device_id={"ctx": lax.rem(me + i, n)}, device_id_type=MESH
+        )
+
+    xbuf[me] = hidden_ref[...]
+    pl.semaphore_wait(barrier, n - 1)
+
+    other_core = me + 1 - 2 * (me % 2)
+    other_y = me + 2 - 4 * ((me // 2) % 2)
+    other_both = other_y + 1 - 2 * (other_y % 2)
+    z_steps = n // 4
+
+    def along_z(base, i):
+        return lax.rem(base + 4 * i, n)
+
+    def block_copy(buf, phase, block, target, k):
+        return pltpu.make_async_remote_copy(
+            src_ref=buf.at[block],
+            dst_ref=buf.at[block],
+            send_sem=send_sem.at[phase, k],
+            recv_sem=recv_sem.at[phase, block],
+            device_id={"ctx": target},
+            device_id_type=MESH,
+        )
+
+    def await_block(buf, phase, block):
+        block_copy(buf, phase, block, other_core, 0).wait_recv()
+
+    def gather(buf, phase):
+        for i in range(1, z_steps):
+            block_copy(buf, phase, me, along_z(me, i), i - 1).start()
+        k = z_steps - 1
+        block_copy(buf, phase, me, other_y, k).start()
+        block_copy(buf, phase, me, other_core, k + 1).start()
+        k += 2
+        for i in range(1, z_steps):
+            block = along_z(me, n // 4 - i)
+            await_block(buf, phase, block)
+            block_copy(buf, phase, block, other_y, k).start()
+            block_copy(buf, phase, block, other_core, k + 1).start()
+            k += 2
+        for i in range(z_steps):
+            block = along_z(other_y, (z_steps - i) % z_steps)
+            await_block(buf, phase, block)
+            block_copy(buf, phase, block, other_core, k).start()
+            k += 1
+        for i in range(z_steps):
+            await_block(buf, phase, along_z(other_core, (z_steps - i) % z_steps))
+        for i in range(z_steps):
+            await_block(buf, phase, along_z(other_both, (z_steps - i) % z_steps))
+
+    def finish_sends(buf, phase):
+        @pl.loop(0, n - 1)
+        def _(k):
+            block_copy(buf, phase, me, other_core, k).wait_send()
+
+    def normalise(buf, gain_ref):
+        width = buf.shape[2]
+
+        def add(s, total):
+            x = buf[s].astype(F32)
+            return total + x * x
+
+        squares = lax.fori_loop(0, n, add, jnp.zeros((rows, width), F32), unroll=4)
+        mean = jnp.sum(squares, axis=1, keepdims=True) / (width * n)
+        factor = lax.rsqrt(mean + NORM_EPSILON)
+
+        @pl.loop(0, n, unroll=4)
+        def _(s):
+            nbuf[s] = (buf[s].astype(F32) * factor * gain_ref[s]).astype(BF16)
+
+    def product(buf, weight):
+        def add(s, total):
+            return total + dot(buf[s], weight[s])
+
+        return lax.fori_loop(0, n, add, jnp.zeros((rows, weight.shape[2]), F32), unroll=4)
+
+    gather(xbuf, 0)
+    normalise(xbuf, again_ref)
+    loads[0].wait()
+    q_part = product(nbuf, wq)
+    cosine, sine = table_ref[0], table_ref[1]
+    for h in range(own_heads):
+        cols = slice(h * head_dim, (h + 1) * head_dim)
+        qbuf[me, :, cols] = turn(q_part[:, cols], cosine, sine).astype(BF16)
+    loads[1].wait()
+    loads[2].wait()
+    kv_part = jnp.zeros((rows, 2 * k_width), F32)
+    width = nbuf.shape[2]
+    for s in range(n):
+        kv_part += dot_nt(nbuf[s], wkv[:, s * width : (s + 1) * width])
+    kv_part = jnp.concatenate(
+        [kv_part, jnp.zeros((rows, head_dim - 2 * k_width), F32)], axis=1
+    )
+    qbuf[me, :, q_width:] = turn(kv_part, table_ref[2], table_ref[3]).astype(BF16)
+    gather(qbuf, 1)
+
+    loads[3].wait()
+    loads[4].wait()
+    lane = lax.broadcasted_iota(jnp.int32, (rows, head_dim), 1)
+    place = place_ref[...]
+    limit = jnp.concatenate([place] * group, axis=0)[:, 0:1]
+    at = me * span + lax.broadcasted_iota(jnp.int32, (group * rows, span), 1)
+    visible = at < limit
+
+    def part_copy(target, source):
+        return pltpu.make_async_remote_copy(
+            src_ref=asend.at[target],
+            dst_ref=arecv.at[source],
+            send_sem=send_sem.at[2, target],
+            recv_sem=recv_sem.at[2, source],
+            device_id={"ctx": target},
+            device_id_type=MESH,
+        )
+
+    for g in range(kv_heads):
+        query = jnp.concatenate(
+            [
+                qbuf[h // own_heads, :, (h % own_heads) * head_dim : (h % own_heads + 1) * head_dim]
+                for h in range(g * group, (g + 1) * group)
+            ],
+            axis=0,
+        )
+        logits = jnp.where(visible, dot_nt(query, keys[g]) * scale, MASKED)
+        top = jnp.max(logits, axis=1, keepdims=True)
+        weights = jnp.where(visible, jnp.exp(logits - top), 0.0)
+        total = jnp.sum(weights, axis=1, keepdims=True)
+        accum = dot(weights.astype(BF16), values[g]).astype(BF16)
+        terms = three_terms(top) + three_terms(total)
+        for d in range(group // own_heads):
+            target = g * (group // own_heads) + d
+            stats = jnp.zeros((rows, head_dim), F32)
+            for h in range(own_heads):
+                j = d * own_heads + h
+                these = slice(j * rows, (j + 1) * rows)
+                asend[target, h * rows : (h + 1) * rows, :] = accum[these]
+                for t, term in enumerate(terms):
+                    stats = jnp.where(lane == h * stat_lanes + t, term[these], stats)
+            asend[target, own_heads * rows :, :] = stats.astype(BF16)
+
+            @pl.when(me != target)
+            def _():
+                part_copy(target, me).start()
+
+    arecv[me] = asend[me]
+
+    @pl.loop(1, n)
+    def _(i):
+        part_copy(0, lax.rem(me + i, n)).wait_recv()
+
+    def stats_of(s):
+        x = arecv[s, own_heads * rows :, :].astype(F32)
+        return x + pltpu.roll(x, head_dim - 1, 1) + pltpu.roll(x, head_dim - 2, 1)
+
+    tops = lax.fori_loop(
+        1, n, lambda s, top: jnp.maximum(top, stats_of(s)), stats_of(0), unroll=5
+    )
+
+    def merge(s, state):
+        stats = stats_of(s)
+        share = jnp.exp(stats - tops)
+        total = state[0] + pltpu.roll(stats, head_dim - 3, 1) * share
+        accums = tuple(
+            state[1 + h]
+            + arecv[s, h * rows : (h + 1) * rows, :].astype(F32)
+            * share[:, h * stat_lanes : h * stat_lanes + 1]
+            for h in range(own_heads)
+        )
+        return (total, *accums)
+
+    zero = jnp.zeros((rows, head_dim), F32)
+    totals, *accums = lax.fori_loop(0, n, merge, (zero,) * (1 + own_heads), unroll=4)
+
+    pieces = head_dim // k_width
+    first_piece = (me * own_heads // group) * pieces
+    key_new, value_new = zero, zero
+    for i in range(pieces):
+        piece = qbuf[first_piece + i, :, q_width:].astype(F32)
+        key_piece = jnp.where(lane < k_width, piece, 0.0)
+        value_piece = jnp.where((lane >= k_width) & (lane < 2 * k_width), piece, 0.0)
+        key_new += pltpu.roll(key_piece, i * k_width, 1) if i else key_piece
+        shift = (i * k_width - k_width) % head_dim
+        value_new += pltpu.roll(value_piece, shift, 1) if shift else value_piece
+    for h in range(own_heads):
+        cols = slice(h * head_dim, (h + 1) * head_dim)
+        at_stat = slice(h * stat_lanes, h * stat_lanes + 1)
+        query = qbuf[me, :, cols].astype(F32)
+        own_score = jnp.sum(query * key_new, axis=1, keepdims=True) * scale
+        top = tops[:, at_stat]
+        peak = jnp.maximum(top, own_score)
+        kept, fresh = jnp.exp(top - peak), jnp.exp(own_score - peak)
+        below = totals[:, at_stat] * kept + fresh
+        abuf[me, :, cols] = ((accums[h] * kept + fresh * value_new) / below).astype(BF16)
+    gather(abuf, 3)
+
+    loads[5].wait()
+    mid = (hidden_ref[...].astype(F32) + product(abuf, wo)).astype(BF16)
+    mbuf[me] = mid
+    gather(mbuf, 4)
+    normalise(mbuf, fgain_ref)
+    loads[6].wait()
+    gate = product(nbuf, wg)
+    loads[7].wait()
+    up = product(nbuf, wu)
+    hbuf[me] = (gate / (1.0 + jnp.exp(-gate)) * up).astype(BF16)
+    gather(hbuf, 5)
+    loads[8].wait()
+    out_ref[...] = (mid.astype(F32) + product(hbuf, wd)).astype(BF16)
+
+    finish_sends(xbuf, 0)
+    finish_sends(qbuf, 1)
+
+    @pl.loop(1, n)
+    def _(i):
+        part_copy(lax.rem(me + i, n), 0).wait_send()
+
+    finish_sends(abuf, 3)
+    finish_sends(mbuf, 4)
+    finish_sends(hbuf, 5)
+
+
+def angle_tables(positions, device, key_width, head_dim):
+    lane = jnp.arange(2 * head_dim, dtype=jnp.int32)
+    second = lane >= head_dim
+    col = jnp.where(second, lane + device * key_width, lane) % head_dim
+    frequency = jnp.exp(
+        -((col - col % 2).astype(F32) / head_dim) * jnp.log(jnp.float32(ROPE_BASE))
+    )
+    turned = ~second | (lane < head_dim + key_width)
+    angles = positions.astype(F32)[:, None] * jnp.where(turned, frequency, 0.0)[None, :]
+    sign = jnp.where(lane % 2 == 0, -1.0, 1.0)
+    cosine, sine = jnp.cos(angles), jnp.sin(angles) * sign[None, :]
+    return jnp.stack(
+        [cosine[:, :head_dim], sine[:, :head_dim], cosine[:, head_dim:], sine[:, head_dim:]]
+    )
+
+
+def shards(
+    hidden_in,
+    attn_gain,
+    w_query,
+    w_key,
+    w_value,
+    rotated_prefix_keys,
+    cache_values,
+    w_out,
+    ffn_gain,
+    w_gate,
+    w_up,
+    w_down,
+    doc_offsets,
+    slot_request,
+):
+    n = lax.axis_size("ctx")
+    device = lax.axis_index("ctx")
+    rows, width = hidden_in.shape
+    span, kv_heads, head_dim = rotated_prefix_keys.shape
+    q_width, k_width = w_query.shape[1], w_key.shape[1]
+    ff_width = w_gate.shape[1]
+    slot_index = jnp.arange(rows, dtype=jnp.int32)
+    positions = jnp.sum(
+        jnp.where(slot_request[:, None] == slot_index[None, :], doc_offsets[None, :], 0), axis=1
+    )
+    tables = angle_tables(positions, device, k_width, head_dim)
+    place = jnp.broadcast_to(positions[:, None], (rows, head_dim))
+    own_heads = q_width // head_dim
+    vmem = pl.BlockSpec(memory_space=pltpu.VMEM)
+    hbm = pl.BlockSpec(memory_space=pl.ANY)
+    weight_shapes = [
+        (n, width, q_width),
+        (2 * k_width, width * n),
+        (kv_heads, span, head_dim),
+        (kv_heads, span, head_dim),
+        (n, q_width, width),
+        (n, width, ff_width),
+        (n, width, ff_width),
+        (n, ff_width, width),
+    ]
+    block_shapes = [
+        (n, rows, width),
+        (n, rows, q_width + head_dim),
+        (n, (own_heads + 1) * rows, head_dim),
+        (n, (own_heads + 1) * rows, head_dim),
+        (n, rows, q_width),
+        (n, rows, width),
+        (n, rows, ff_width),
+        (n, rows, width),
+    ]
+    return pl.pallas_call(
+        functools.partial(layer_kernel, n),
+        out_shape=jax.ShapeDtypeStruct((rows, width), BF16),
+        in_specs=[vmem] * 5 + [hbm] * 9,
+        out_specs=vmem,
+        scratch_shapes=[pltpu.VMEM(shape, BF16) for shape in weight_shapes + block_shapes]
+        + [
+            pltpu.SemaphoreType.DMA((9,)),
+            pltpu.SemaphoreType.DMA((6, n)),
+            pltpu.SemaphoreType.DMA((6, n)),
+        ],
+        compiler_params=pltpu.CompilerParams(
+            collective_id=0, has_side_effects=True, vmem_limit_bytes=62 * 1024 * 1024
+        ),
+        name="layer",
+    )(
+        hidden_in,
+        attn_gain.reshape(n, 1, width),
+        ffn_gain.reshape(n, 1, width),
+        tables,
+        place,
+        w_query.reshape(n, width, q_width),
+        w_key.T,
+        w_value.T,
+        jnp.transpose(rotated_prefix_keys, (1, 0, 2)),
+        jnp.transpose(cache_values, (1, 0, 2)),
+        w_out.reshape(n, q_width, width),
+        w_gate.reshape(n, width, ff_width),
+        w_up.reshape(n, width, ff_width),
+        w_down.reshape(n, ff_width, width),
+    )
+
+
+def pick(*arrays):
+    n = lax.axis_size("ctx")
+    rows, width = arrays[0].shape
+    span, kv_heads, head_dim = arrays[5].shape
+    q_width, k_width, ff_width = arrays[2].shape[1], arrays[3].shape[1], arrays[9].shape[1]
+    whole_tiles = (
+        n % 4 == 0
+        and n >= 8
+        and head_dim == 128
+        and rows % 16 == 0
+        and all(w % 128 == 0 for w in (width, q_width, ff_width, span))
+        and k_width % 16 == 0
+        and 2 * k_width <= head_dim
+        and head_dim % k_width == 0
+    )
+    if not whole_tiles:
+        return plain_shards(*arrays)
+    own_heads = q_width // head_dim
+    group = own_heads * n // kv_heads
+    if group % own_heads or own_heads > 8:
+        return plain_shards(*arrays)
+    return shards(*arrays)
+
+
 def solution(mesh):
     return jax.shard_map(
-        shards,
+        pick,
         mesh=mesh,
         in_specs=(
             P("groups", "ctx"),

time: 230 us -> 72.9 us (0.32)
  blocking collectives: 161 us -> 0 us
  Pallas kernels: 0 us -> 65.6 us
  matrix products: 24.2 us -> 0 us
  other arithmetic: 21.2 us -> 1.65 us
  between operations: 13.7 us -> 0.03 us
  local copies, waits for them, and re-layouts: 8.55 us -> 5.16 us
    all_gather x8 -> x0, blocking collectives: 161 us -> none  [the longest x2 39.9 us: joined(): gathered = jax.tree.map(lambda a: lax.all_gather(a, axis), part)]
    pallas_call x0 -> x1, Pallas kernels: none -> 65.6 us  [shards(): pl.pallas_call(functools.partial(layer_kernel, n), out_shape=jax.ShapeDty...]
    dot_general x10 -> x0, matrix products: 24.2 us -> none  [the longest x1 7.36 us: shards(): gate_act = jnp.dot(normed_mid, w_gate, preferred_element_type=jnp.float32)]
    add x32 -> x0, other arithmetic: 18.6 us -> none  [the longest x15 18.2 us: combine_parts(): accum_first * share_first[..., None]]
    transpose x0 -> x1, local copies, waits for them, and re-layouts: none -> 3.16 us  [shards(): jnp.transpose(cache_values, (1, 0, 2))]
    exp x32 -> x0, local copies, waits for them, and re-layouts: 2.49 us -> none  [the longest x15 1.18 us: combine_parts(): share_second = jnp.exp(top_second - peak_score)]
  transfers between devices with their start and end apart: 1 -> 0, of which waited for: 0 -> 0; matrix products, arithmetic and copies ran while one was open for 2% -> 0% of each run, Pallas kernels for 0% -> 0%
where the time goes in v1:
time: 72.9 us; the launch traced here: 72.4 us
  Pallas kernels  65.6 us (90%)
  local copies, waits for them, and re-layouts  5.16 us (7%)
  other arithmetic  1.65 us (2%)
    pallas_call x1, Pallas kernels, shards(): pl.pallas_call(functools.partial(layer_kernel, n), out_shape=jax.ShapeDty...  65.6 us
    transpose x1, local copies, waits for them, and re-layouts, shards(): jnp.transpose(cache_values, (1, 0, 2))  3.16 us

profile of v1, /device:TPU:0, one launch (start us, length us, event | category | flops | bytes accessed | tf_op | source)
XLA Modules:
  0.0 72.4 jit_solution(15895964010462367541)
XLA Ops:
  0.0 0.9 %select_reduce_fusion = s32[16]{0:T(128)S(1)} fusion(s32[16]{0:T(128)} %param.26, s32[16]{0:T(128)} %param.27), kind=kLoop, calls=%fused_computation.10 | loop fusion | flops 752 | bytes 192 | tf_op jit(solution)/shard_map/reduce_sum | solution.py:538
  0.9 0.7 broadcast_in_dim.41.place_ref
  1.6 0.1 multiply_cosine_fusion
  1.7 0.6 pad_maximum_fusion.table_ref
  2.3 3.2 %copy_bitcast_fusion = (bf16[4,1024,128]{2,1,0:T(8,128)(2,1)}, bf16[4,1024,128]{2,1,0:T(8,128)(2,1)}) fusion(bf16[1024,4,128]{2,1,0:T(4,128)(2,1)} %param.20, bf16[1024,4,128]{2,1,0:T(4,128)(2,1)} %param.19), kind=kLoop, calls=%fused_computation | loop fusion | bytes 4194304 | tf_op jit(solution)/shard_map/transpose | solution.py:591
  5.5 65.6 %layer.1 = bf16[16,512]{1,0:T(8,128)(2,1)} custom-call(bf16[16,512]{1,0:T(8,128)(2,1)} %hidden_ref.1, f32[16,1,512]{2,1,0:T(1,128)} %bitcast.28, f32[16,1,512]{2,1,0:T(1,128)} %bitcast.29, f32[4,16,128]{2,1,0:T(8,128)} %pad_maximum_fusion.table_ref, s32[16,128]{1,0:T(8,128)} %broadcast_in_dim.41.place_ref, bf16[16,512,256]{2,1,0:T(8,128)(2,1)} %bitcast.24, ...), custom_call_target="tpu_custom_call" | custom-call | tf_op jit(solution)/shard_map/layer/pallas_call | solution.py:566
  71.1 1.3 %copy.22 = bf16[16,512]{1,0:T(8,128)(2,1)} copy(bf16[16,512]{1,0:T(8,128)(2,1)} %layer.1) | data formatting | bytes 32768
  (4 shorter events, 0.0 us)

commit v2 on v1

--- a/solution.py
+++ b/solution.py
@@ -236,7 +236,6 @@
     abuf,
     mbuf,
     hbuf,
-    nbuf,
     local_sem,
     send_sem,
     recv_sem,
@@ -279,98 +278,108 @@
             barrier, inc=1, device_id={"ctx": lax.rem(me + i, n)}, device_id_type=MESH
         )
 
-    xbuf[me] = hidden_ref[...]
+    low, z, z_steps = me % 4, me // 4, n // 4
+    xbuf[low, z] = hidden_ref[...]
     pl.semaphore_wait(barrier, n - 1)
 
     other_core = me + 1 - 2 * (me % 2)
     other_y = me + 2 - 4 * ((me // 2) % 2)
     other_both = other_y + 1 - 2 * (other_y % 2)
-    z_steps = n // 4
-
-    def along_z(base, i):
-        return lax.rem(base + 4 * i, n)
-
-    def block_copy(buf, phase, block, target, k):
+
+    def block_copy(buf, phase, from_z, target, k):
         return pltpu.make_async_remote_copy(
-            src_ref=buf.at[block],
-            dst_ref=buf.at[block],
+            src_ref=buf.at[low, from_z],
+            dst_ref=buf.at[low, from_z],
             send_sem=send_sem.at[phase, k],
-            recv_sem=recv_sem.at[phase, block],
+            recv_sem=recv_sem.at[phase, from_z],
             device_id={"ctx": target},
             device_id_type=MESH,
         )
 
-    def await_block(buf, phase, block):
-        block_copy(buf, phase, block, other_core, 0).wait_recv()
+    def set_copy(buf, phase, which, target, k):
+        return pltpu.make_async_remote_copy(
+            src_ref=buf.at[which],
+            dst_ref=buf.at[which],
+            send_sem=send_sem.at[phase, z_steps - 1 + k],
+            recv_sem=recv_sem.at[phase, z_steps + which],
+            device_id={"ctx": target},
+            device_id_type=MESH,
+        )
 
     def gather(buf, phase):
         for i in range(1, z_steps):
-            block_copy(buf, phase, me, along_z(me, i), i - 1).start()
-        k = z_steps - 1
-        block_copy(buf, phase, me, other_y, k).start()
-        block_copy(buf, phase, me, other_core, k + 1).start()
-        k += 2
+            block_copy(buf, phase, z, lax.rem(me + 4 * i, n), i - 1).start()
         for i in range(1, z_steps):
-            block = along_z(me, n // 4 - i)
-            await_block(buf, phase, block)
-            block_copy(buf, phase, block, other_y, k).start()
-            block_copy(buf, phase, block, other_core, k + 1).start()
-            k += 2
-        for i in range(z_steps):
-            block = along_z(other_y, (z_steps - i) % z_steps)
-            await_block(buf, phase, block)
-            block_copy(buf, phase, block, other_core, k).start()
-            k += 1
-        for i in range(z_steps):
-            await_block(buf, phase, along_z(other_core, (z_steps - i) % z_steps))
-        for i in range(z_steps):
-            await_block(buf, phase, along_z(other_both, (z_steps - i) % z_steps))
+            block_copy(buf, phase, lax.rem(z + i, z_steps), other_core, 0).wait_recv()
+        for k, peer in enumerate((other_both, other_y, other_core)):
+            set_copy(buf, phase, low, peer, k).start()
+        yield low
+        for peer in (other_core, other_y, other_both):
+            which = peer % 4
+            set_copy(buf, phase, which, other_core, 0).wait_recv()
+            yield which
+
+    def gather_all(buf, phase):
+        for _ in gather(buf, phase):
+            pass
 
     def finish_sends(buf, phase):
-        @pl.loop(0, n - 1)
-        def _(k):
-            block_copy(buf, phase, me, other_core, k).wait_send()
-
-    def normalise(buf, gain_ref):
-        width = buf.shape[2]
-
-        def add(s, total):
-            x = buf[s].astype(F32)
-            return total + x * x
-
-        squares = lax.fori_loop(0, n, add, jnp.zeros((rows, width), F32), unroll=4)
-        mean = jnp.sum(squares, axis=1, keepdims=True) / (width * n)
-        factor = lax.rsqrt(mean + NORM_EPSILON)
-
-        @pl.loop(0, n, unroll=4)
-        def _(s):
-            nbuf[s] = (buf[s].astype(F32) * factor * gain_ref[s]).astype(BF16)
-
-    def product(buf, weight):
-        def add(s, total):
-            return total + dot(buf[s], weight[s])
-
-        return lax.fori_loop(0, n, add, jnp.zeros((rows, weight.shape[2]), F32), unroll=4)
-
-    gather(xbuf, 0)
-    normalise(xbuf, again_ref)
-    loads[0].wait()
-    q_part = product(nbuf, wq)
+        for i in range(1, z_steps):
+            block_copy(buf, phase, z, other_core, i - 1).wait_send()
+        for k in range(3):
+            set_copy(buf, phase, low, other_core, k).wait_send()
+
+    def over_set(step, which, state):
+        return lax.fori_loop(
+            0, z_steps, lambda at_z, state: step(which, at_z, at_z * 4 + which, state), state,
+            unroll=True,
+        )
+
+    def row_factor(squares):
+        mean = jnp.sum(squares, axis=1, keepdims=True) / (squares.shape[1] * n)
+        return lax.rsqrt(mean + NORM_EPSILON)
+
+    def product(buf, phase, load, weight):
+        def add(which, at_z, source, total):
+            return total + dot(buf[which, at_z], weight[source])
+
+        total = jnp.zeros((rows, weight.shape[2]), F32)
+        for step, which in enumerate(gather(buf, phase)):
+            if step == 0:
+                load.wait()
+            total = over_set(add, which, total)
+        return total
+
+    width = xbuf.shape[3]
+
+    def project_in(which, at_z, source, state):
+        squares, q_part, kv_part = state
+        x = xbuf[which, at_z].astype(F32)
+        scaled = (x * again_ref[source]).astype(BF16)
+        cols = pl.ds(pl.multiple_of(source * width, width), width)
+        return (
+            squares + x * x,
+            q_part + dot(scaled, wq[source]),
+            kv_part + dot_nt(scaled, wkv[:, cols]),
+        )
+
+    state = tuple(jnp.zeros((rows, w), F32) for w in (width, q_width, 2 * k_width))
+    for step, which in enumerate(gather(xbuf, 0)):
+        if step == 0:
+            for load in loads[:3]:
+                load.wait()
+        state = over_set(project_in, which, state)
+    factor = row_factor(state[0])
+    q_part, kv_part = state[1] * factor, state[2] * factor
     cosine, sine = table_ref[0], table_ref[1]
     for h in range(own_heads):
         cols = slice(h * head_dim, (h + 1) * head_dim)
-        qbuf[me, :, cols] = turn(q_part[:, cols], cosine, sine).astype(BF16)
-    loads[1].wait()
-    loads[2].wait()
-    kv_part = jnp.zeros((rows, 2 * k_width), F32)
-    width = nbuf.shape[2]
-    for s in range(n):
-        kv_part += dot_nt(nbuf[s], wkv[:, s * width : (s + 1) * width])
+        qbuf[low, z, :, cols] = turn(q_part[:, cols], cosine, sine).astype(BF16)
     kv_part = jnp.concatenate(
         [kv_part, jnp.zeros((rows, head_dim - 2 * k_width), F32)], axis=1
     )
-    qbuf[me, :, q_width:] = turn(kv_part, table_ref[2], table_ref[3]).astype(BF16)
-    gather(qbuf, 1)
+    qbuf[low, z, :, q_width:] = turn(kv_part, table_ref[2], table_ref[3]).astype(BF16)
+    gather_all(qbuf, 1)
 
     loads[3].wait()
     loads[4].wait()
@@ -393,8 +402,9 @@
     for g in range(kv_heads):
         query = jnp.concatenate(
             [
-                qbuf[h // own_heads, :, (h % own_heads) * head_dim : (h % own_heads + 1) * head_dim]
-                for h in range(g * group, (g + 1) * group)
+                qbuf[d % 4, d // 4, :, h * head_dim : (h + 1) * head_dim]
+                for d in range(g * group // own_heads, (g + 1) * group // own_heads)
+                for h in range(own_heads)
             ],
             axis=0,
         )
@@ -452,7 +462,8 @@
     first_piece = (me * own_heads // group) * pieces
     key_new, value_new = zero, zero
     for i in range(pieces):
-        piece = qbuf[first_piece + i, :, q_width:].astype(F32)
+        source = first_piece + i
+        piece = qbuf[source % 4, source // 4, :, q_width:].astype(F32)
         key_piece = jnp.where(lane < k_width, piece, 0.0)
         value_piece = jnp.where((lane >= k_width) & (lane < 2 * k_width), piece, 0.0)
         key_new += pltpu.roll(key_piece, i * k_width, 1) if i else key_piece
@@ -461,28 +472,39 @@
     for h in range(own_heads):
         cols = slice(h * head_dim, (h + 1) * head_dim)
         at_stat = slice(h * stat_lanes, h * stat_lanes + 1)
-        query = qbuf[me, :, cols].astype(F32)
+        query = qbuf[low, z, :, cols].astype(F32)
         own_score = jnp.sum(query * key_new, axis=1, keepdims=True) * scale
         top = tops[:, at_stat]
         peak = jnp.maximum(top, own_score)
         kept, fresh = jnp.exp(top - peak), jnp.exp(own_score - peak)
         below = totals[:, at_stat] * kept + fresh
-        abuf[me, :, cols] = ((accums[h] * kept + fresh * value_new) / below).astype(BF16)
-    gather(abuf, 3)
-
-    loads[5].wait()
-    mid = (hidden_ref[...].astype(F32) + product(abuf, wo)).astype(BF16)
-    mbuf[me] = mid
-    gather(mbuf, 4)
-    normalise(mbuf, fgain_ref)
-    loads[6].wait()
-    gate = product(nbuf, wg)
-    loads[7].wait()
-    up = product(nbuf, wu)
-    hbuf[me] = (gate / (1.0 + jnp.exp(-gate)) * up).astype(BF16)
-    gather(hbuf, 5)
-    loads[8].wait()
-    out_ref[...] = (mid.astype(F32) + product(hbuf, wd)).astype(BF16)
+        abuf[low, z, :, cols] = ((accums[h] * kept + fresh * value_new) / below).astype(BF16)
+
+    attn_part = product(abuf, 3, loads[5], wo)
+    mid = (hidden_ref[...].astype(F32) + attn_part).astype(BF16)
+    mbuf[low, z] = mid
+
+    def feed(which, at_z, source, state):
+        squares, gate, up = state
+        x = mbuf[which, at_z].astype(F32)
+        scaled = (x * fgain_ref[source]).astype(BF16)
+        return (
+            squares + x * x,
+            gate + dot(scaled, wg[source]),
+            up + dot(scaled, wu[source]),
+        )
+
+    ff_width = wg.shape[2]
+    state = tuple(jnp.zeros((rows, w), F32) for w in (width, ff_width, ff_width))
+    for step, which in enumerate(gather(mbuf, 4)):
+        if step == 0:
+            loads[6].wait()
+            loads[7].wait()
+        state = over_set(feed, which, state)
+    factor = row_factor(state[0])
+    gate, up = state[1] * factor, state[2] * factor
+    hbuf[low, z] = (gate / (1.0 + jnp.exp(-gate)) * up).astype(BF16)
+    out_ref[...] = (mid.astype(F32) + product(hbuf, 5, loads[8], wd)).astype(BF16)
 
     finish_sends(xbuf, 0)
     finish_sends(qbuf, 1)
@@ -554,14 +576,13 @@
         (n, ff_width, width),
     ]
     block_shapes = [
-        (n, rows, width),
-        (n, rows, q_width + head_dim),
+        (4, n // 4, rows, width),
+        (4, n // 4, rows, q_width + head_dim),
         (n, (own_heads + 1) * rows, head_dim),
         (n, (own_heads + 1) * rows, head_dim),
-        (n, rows, q_width),
-        (n, rows, width),
-        (n, rows, ff_width),
-        (n, rows, width),
+        (4, n // 4, rows, q_width),
+        (4, n // 4, rows, width),
+        (4, n // 4, rows, ff_width),
     ]
     return pl.pallas_call(
         functools.partial(layer_kernel, n),

time: 72.9 us -> 68.4 us (0.938)
  Pallas kernels: 65.6 us -> 61.3 us
    pallas_call x1, Pallas kernels: 65.6 us -> 61.3 us  [shards(): pl.pallas_call(functools.partial(layer_kernel, n), out_shape=jax.ShapeDty...]
where the time goes in v2:
time: 68.4 us; the launch traced here: 68.2 us
  Pallas kernels  61.3 us (90%)
  local copies, waits for them, and re-layouts  5.16 us (8%)
  other arithmetic  1.65 us (2%)
    pallas_call x1, Pallas kernels, shards(): pl.pallas_call(functools.partial(layer_kernel, n), out_shape=jax.ShapeDty...  61.3 us
    transpose x1, local copies, waits for them, and re-layouts, shards(): jnp.transpose(cache_values, (1, 0, 2))  3.16 us

profile of v2, /device:TPU:0, one launch (start us, length us, event | category | flops | bytes accessed | tf_op | source)
XLA Modules:
  0.0 68.2 jit_solution(18151480943730130279)
XLA Ops:
  0.0 0.9 %select_reduce_fusion = s32[16]{0:T(128)S(1)} fusion(s32[16]{0:T(128)} %param.26, s32[16]{0:T(128)} %param.27), kind=kLoop, calls=%fused_computation.10 | loop fusion | flops 752 | bytes 192 | tf_op jit(solution)/shard_map/reduce_sum | solution.py:560
  0.9 0.7 broadcast_in_dim.41.place_ref
  1.6 0.1 multiply_cosine_fusion
  1.7 0.6 pad_maximum_fusion.table_ref
  2.3 3.2 %copy_bitcast_fusion = (bf16[4,1024,128]{2,1,0:T(8,128)(2,1)}, bf16[4,1024,128]{2,1,0:T(8,128)(2,1)}) fusion(bf16[1024,4,128]{2,1,0:T(4,128)(2,1)} %param.20, bf16[1024,4,128]{2,1,0:T(4,128)(2,1)} %param.19), kind=kLoop, calls=%fused_computation | loop fusion | bytes 4194304 | tf_op jit(solution)/shard_map/transpose | solution.py:612
  5.5 61.3 %layer.1 = bf16[16,512]{1,0:T(8,128)(2,1)} custom-call(bf16[16,512]{1,0:T(8,128)(2,1)} %hidden_ref.1, f32[16,1,512]{2,1,0:T(1,128)} %bitcast.28, f32[16,1,512]{2,1,0:T(1,128)} %bitcast.29, f32[4,16,128]{2,1,0:T(8,128)} %pad_maximum_fusion.table_ref, s32[16,128]{1,0:T(8,128)} %broadcast_in_dim.41.place_ref, bf16[16,512,256]{2,1,0:T(8,128)(2,1)} %bitcast.24, ...), custom_call_target="tpu_custom_call" | custom-call | tf_op jit(solution)/shard_map/layer/pallas_call | solution.py:587
  66.8 1.3 %copy.22 = bf16[16,512]{1,0:T(8,128)(2,1)} copy(bf16[16,512]{1,0:T(8,128)(2,1)} %layer.1) | data formatting | bytes 32768
  (4 shorter events, 0.0 us)

commit v3 on v2

--- a/solution.py
+++ b/solution.py
@@ -286,37 +286,33 @@
     other_y = me + 2 - 4 * ((me // 2) % 2)
     other_both = other_y + 1 - 2 * (other_y % 2)
 
-    def block_copy(buf, phase, from_z, target, k):
+    def block_copy(buf, phase, which, from_z, target, k):
         return pltpu.make_async_remote_copy(
-            src_ref=buf.at[low, from_z],
-            dst_ref=buf.at[low, from_z],
+            src_ref=buf.at[which, from_z],
+            dst_ref=buf.at[which, from_z],
             send_sem=send_sem.at[phase, k],
-            recv_sem=recv_sem.at[phase, from_z],
+            recv_sem=recv_sem.at[phase, from_z * 4 + which],
             device_id={"ctx": target},
             device_id_type=MESH,
         )
 
-    def set_copy(buf, phase, which, target, k):
-        return pltpu.make_async_remote_copy(
-            src_ref=buf.at[which],
-            dst_ref=buf.at[which],
-            send_sem=send_sem.at[phase, z_steps - 1 + k],
-            recv_sem=recv_sem.at[phase, z_steps + which],
-            device_id={"ctx": target},
-            device_id_type=MESH,
-        )
-
     def gather(buf, phase):
+        plane = (other_both, other_y, other_core)
         for i in range(1, z_steps):
-            block_copy(buf, phase, z, lax.rem(me + 4 * i, n), i - 1).start()
-        for i in range(1, z_steps):
-            block_copy(buf, phase, lax.rem(z + i, z_steps), other_core, 0).wait_recv()
-        for k, peer in enumerate((other_both, other_y, other_core)):
-            set_copy(buf, phase, low, peer, k).start()
+            block_copy(buf, phase, low, z, lax.rem(me + 4 * i, n), i - 1).start()
+        k = z_steps - 1
+        for i in range(z_steps):
+            from_z = lax.rem(z + i, z_steps)
+            if i:
+                block_copy(buf, phase, low, from_z, other_core, 0).wait_recv()
+            for peer in plane:
+                block_copy(buf, phase, low, from_z, peer, k).start()
+                k += 1
         yield low
         for peer in (other_core, other_y, other_both):
             which = peer % 4
-            set_copy(buf, phase, which, other_core, 0).wait_recv()
+            for i in range(z_steps):
+                block_copy(buf, phase, which, lax.rem(z + i, z_steps), other_core, 0).wait_recv()
             yield which
 
     def gather_all(buf, phase):
@@ -324,10 +320,9 @@
             pass
 
     def finish_sends(buf, phase):
-        for i in range(1, z_steps):
-            block_copy(buf, phase, z, other_core, i - 1).wait_send()
-        for k in range(3):
-            set_copy(buf, phase, low, other_core, k).wait_send()
+        @pl.loop(0, n - 1)
+        def _(k):
+            block_copy(buf, phase, low, z, other_core, k).wait_send()
 
     def over_set(step, which, state):
         return lax.fori_loop(

time: 68.4 us -> 65.9 us (0.963)
  Pallas kernels: 61.3 us -> 58.8 us
    pallas_call x1, Pallas kernels: 61.3 us -> 58.8 us  [shards(): pl.pallas_call(functools.partial(layer_kernel, n), out_shape=jax.ShapeDty...]
where the time goes in v3:
time: 65.9 us; the launch traced here: 65.6 us
  Pallas kernels  58.8 us (89%)
  local copies, waits for them, and re-layouts  5.16 us (8%)
  other arithmetic  1.65 us (3%)
    pallas_call x1, Pallas kernels, shards(): pl.pallas_call(functools.partial(layer_kernel, n), out_shape=jax.ShapeDty...  58.8 us
    transpose x1, local copies, waits for them, and re-layouts, shards(): jnp.transpose(cache_values, (1, 0, 2))  3.16 us
    unnamed x1, local copies, waits for them, and re-layouts  1.32 us

profile of v3, /device:TPU:0, one launch (start us, length us, event | category | flops | bytes accessed | tf_op | source)
XLA Modules:
  0.0 65.6 jit_solution(8041630031044956177)
XLA Ops:
  0.0 0.9 %select_reduce_fusion = s32[16]{0:T(128)S(1)} fusion(s32[16]{0:T(128)} %param.26, s32[16]{0:T(128)} %param.27), kind=kLoop, calls=%fused_computation.10 | loop fusion | flops 752 | bytes 192 | tf_op jit(solution)/shard_map/reduce_sum | solution.py:555
  0.9 0.7 %broadcast_in_dim.41.place_ref = s32[16,128]{1,0:T(8,128)} broadcast(s32[16]{0:T(128)S(1)} %select_reduce_fusion), dimensions={0} | broadcast | bytes 8256 | tf_op jit(solution)/shard_map/broadcast_in_dim | solution.py:559
  1.6 0.1 multiply_cosine_fusion
  1.7 0.6 pad_maximum_fusion.table_ref
  2.3 3.2 %copy_bitcast_fusion = (bf16[4,1024,128]{2,1,0:T(8,128)(2,1)}, bf16[4,1024,128]{2,1,0:T(8,128)(2,1)}) fusion(bf16[1024,4,128]{2,1,0:T(4,128)(2,1)} %param.20, bf16[1024,4,128]{2,1,0:T(4,128)(2,1)} %param.19), kind=kLoop, calls=%fused_computation | loop fusion | bytes 4194304 | tf_op jit(solution)/shard_map/transpose | solution.py:607
  5.5 58.8 %layer.1 = bf16[16,512]{1,0:T(8,128)(2,1)} custom-call(bf16[16,512]{1,0:T(8,128)(2,1)} %hidden_ref.1, f32[16,1,512]{2,1,0:T(1,128)} %bitcast.28, f32[16,1,512]{2,1,0:T(1,128)} %bitcast.29, f32[4,16,128]{2,1,0:T(8,128)} %pad_maximum_fusion.table_ref, s32[16,128]{1,0:T(8,128)} %broadcast_in_dim.41.place_ref, bf16[16,512,256]{2,1,0:T(8,128)(2,1)} %bitcast.24, ...), custom_call_target="tpu_custom_call" | custom-call | tf_op jit(solution)/shard_map/layer/pallas_call | solution.py:582
  64.3 1.3 %copy.22 = bf16[16,512]{1,0:T(8,128)(2,1)} copy(bf16[16,512]{1,0:T(8,128)(2,1)} %layer.1) | data formatting | bytes 32768
  (4 shorter events, 0.0 us)
